TPU v7x, 32 devices: a whole 2x2x4 slice. The times are simulated.
32 devices in a mesh: ka: 8 (over z, x), ha: 4 (over y, core).
Axes of the slice: x: 2, y: 2, z: 4, core: 2. Of those that a mesh axis runs over, the one named last changes fastest.
Arguments:
- green_row: bfloat16 [64, 256, 64, 128], P('ha', None, 'ka'), may hold values from -6 to 6
- screened: bfloat16 [64, 256, 64, 128], P('ha', 'ka'), may hold values from -6 to 6
- propagator: float32 [256, 64, 128], P(None, 'ka'), may hold values from -1.5 to 1.5
Outputs:
- new_row: bfloat16 [64, 256, 64, 128], P('ha', None, 'ka')
All inputs are finite; a program needn't handle non-finite values.
Results may differ from a plain program's by a relative error of at most 0.008.
Values may be sent and summed in bfloat16 or wider, within the bound.
A program may use at most 512 MiB of HBM per device.

v0:
```python
import math

import jax
import jax.numpy as jnp
from jax import lax
from jax.sharding import PartitionSpec as P

NO = 16
NKX = 64
NKY = 64


step_size = 0.004


def tables(count):
    index = jnp.arange(count, dtype=jnp.int32)
    product = index[:, None] * index[None, :] % count
    angle = product.astype(jnp.float32) * (2.0 * math.pi / count)
    scale = 1.0 / math.sqrt(count)
    return (
        (jnp.cos(angle) * scale).astype(jnp.bfloat16),
        (jnp.sin(angle) * scale).astype(jnp.bfloat16),
    )


def row_matrix(cosine, sine, forward):
    signed = sine if forward else -sine
    upper = jnp.concatenate([cosine, signed], axis=1)
    lower = jnp.concatenate([-signed, cosine], axis=1)
    return jnp.concatenate([upper, lower], axis=0)


def on_device(green_row, screened, propagator):
    steps_local, pairs, rows_local, columns = green_row.shape
    half_width = columns // 2
    cos_y, sin_y = tables(NKY)
    cos_x, sin_x = tables(NKX)
    forward_y = row_matrix(cos_y, sin_y, True)
    inverse_y = row_matrix(cos_y, sin_y, False)
    stacked_x = jnp.concatenate([cos_x, sin_x], axis=1)
    count_x = cos_x.shape[0]
    moved = lax.all_to_all(green_row, "ka", split_axis=1, concat_axis=2, tiled=True)
    half = jnp.einsum("spxw,wv->spxv", moved, forward_y, preferred_element_type=jnp.float32).astype(
        jnp.bfloat16
    )
    both = jnp.einsum("spxw,xz->spwz", half, stacked_x, preferred_element_type=jnp.float32)
    first = both[..., :count_x]
    second = both[..., count_x:]
    space_re = first[:, :, :half_width] - second[:, :, half_width:]
    space_im = first[:, :, half_width:] + second[:, :, :half_width]
    screen_turned = jnp.swapaxes(screened, 2, 3).astype(jnp.float32)
    screen_re = screen_turned[:, :, :half_width]
    screen_im = screen_turned[:, :, half_width:]
    product = jnp.concatenate(
        [space_re * screen_re - space_im * screen_im, space_re * screen_im + space_im * screen_re],
        axis=2,
    ).astype(jnp.bfloat16)
    both_back = jnp.einsum("spwz,zx->spwx", product, stacked_x, preferred_element_type=jnp.float32)
    first_back = both_back[..., :count_x]
    second_back = both_back[..., count_x:]
    back = jnp.concatenate(
        [
            first_back[:, :, :half_width] + second_back[:, :, half_width:],
            first_back[:, :, half_width:] - second_back[:, :, :half_width],
        ],
        axis=2,
    ).astype(jnp.bfloat16)
    sigma_pairs = jnp.einsum(
        "spwx,wv->spxv", back, inverse_y, preferred_element_type=jnp.float32
    ).astype(jnp.bfloat16)
    sigma = lax.all_to_all(sigma_pairs, "ka", split_axis=2, concat_axis=1, tiled=True)
    orbital_shape = (steps_local, NO, NO, rows_local, columns)
    sigma = sigma.reshape(orbital_shape)
    green = green_row.reshape(orbital_shape)
    sigma_re = sigma[..., :half_width]
    sigma_im = sigma[..., half_width:]
    green_re = green[..., :half_width]
    green_im = green[..., half_width:]
    form = "uacxw,ubcxw->abxw"

    def contract(left, right):
        return jnp.einsum(form, left, right, preferred_element_type=jnp.float32)

    memory_re = contract(sigma_re, green_re) + contract(sigma_im, green_im)
    memory_im = contract(sigma_im, green_re) - contract(sigma_re, green_im)
    local_memory = -step_size * jnp.concatenate([memory_re, memory_im], axis=-1)
    base = propagator.reshape(NO, NO, rows_local, columns)
    memory = lax.psum(local_memory, "ha")
    kernel = (base - memory).astype(jnp.bfloat16)
    kernel_re = kernel[..., :half_width]
    kernel_im = kernel[..., half_width:]
    apply_form = "abxw,ubcxw->uacxw"

    def apply_kernel(left, right):
        return jnp.einsum(apply_form, left, right, preferred_element_type=jnp.float32)

    new_re = apply_kernel(kernel_re, green_re) - apply_kernel(kernel_im, green_im)
    new_im = apply_kernel(kernel_re, green_im) + apply_kernel(kernel_im, green_re)
    result = jnp.concatenate([new_re, new_im], axis=-1)
    return result.astype(jnp.bfloat16).reshape(steps_local, pairs, rows_local, columns)


def solution(mesh):
    in_specs = (P("ha", None, "ka", None), P("ha", "ka", None, None), P(None, "ka", None))
    out_specs = P("ha", None, "ka", None)
    return jax.shard_map(
        on_device, mesh=mesh, in_specs=in_specs, out_specs=out_specs, check_vma=False
    )
```

profile of v0, /device:TPU:11, one launch (start us, length us, event | category | flops | bytes accessed | tf_op | source)
XLA Modules:
  0.0 1041.3 jit_solution(6500042863061789453)
XLA Ops:
  6.5 9.2 copy.76
  15.7 5.7 all-to-all-start
  21.7 11.3 %convert_bitcast_fusion = f32[16,32,128,64]{2,3,1,0:T(8,128)} fusion(bf16[16,32,64,128]{3,2,1,0:T(8,128)(2,1)} %param.4), kind=kLoop, calls=%fused_computation.10 | loop fusion | flops 4194304 | bytes 25165824 | tf_op jit(solution)/shard_map/convert_element_type | solution.py:52
  33.0 169.0 %all-to-all-done = bf16[16,256,8,128]{3,2,0,1:T(8,128)(2,1)} async-done(((bf16[16,256,8,128]{3,2,0,1:T(8,128)(2,1)}), bf16[16,256,8,128]{3,2,0,1:T(8,128)(2,1)}, u32[]{:S(2)}, u32[]{:S(2)}) %all-to-all-start) | async-done | bytes 8388640 | tf_op jit(solution)/shard_map/all_to_all | solution.py:43
  201.9 15.8 %fusion.12 = f32[16,32,128,128]{2,3,1,0:T(8,128)} fusion(bf16[16,32,8,8,128]{4,3,0,1,2:T(8,128)(2,1)} %bitcast.5, bf16[64,64]{1,0:T(8,128)(2,1)S(1)} %get-tuple-element.16, bf16[64,64]{1,0:T(8,128)(2,1)S(1)} %fusion.46, bf16[64,64]{1,0:T(8,128)(2,1)S(1)} %get-tuple-element.15), kind=kOutput, calls=%fused_computation.22 | convolution fusion | flops 2151841792 | bytes 41967616 | tf_op jit(solution)/shard_map/spxw,xz->spwz/dot_general | solution.py:47
  217.7 40.3 %subtract_convert_fusion.1 = (bf16[16,32,64,64]{2,3,1,0:T(8,128)(2,1)}, bf16[16,32,64,64]{2,3,1,0:T(8,128)(2,1)}) fusion(f32[16,32,128,64]{2,3,1,0:T(8,128)} %convert_bitcast_fusion, f32[16,32,128,128]{2,3,1,0:T(8,128)} %fusion.12), kind=kLoop, calls=%fused_computation.12 | loop fusion | flops 20971520 | bytes 58720256 | tf_op jit(solution)/shard_map/convert.9
  258.0 16.7 %fusion.4 = f32[16,32,128,128]{2,3,1,0:T(8,128)} fusion(bf16[16,32,64,64]{2,3,1,0:T(8,128)(2,1)} %get-tuple-element.6, bf16[16,32,64,64]{2,3,1,0:T(8,128)(2,1)} %get-tuple-element.5, bf16[64,64]{1,0:T(8,128)(2,1)S(1)} %get-tuple-element.15, bf16[64,64]{1,0:T(8,128)(2,1)S(1)} %get-tuple-element.16), kind=kOutput, calls=%fused_computation.13 | convolution fusion | flops 1090551808 | bytes 41959424 | tf_op jit(solution)/shard_map/spwz,zx->spwx/dot_general | solution.py:59
  274.7 26.8 %fusion.3 = (bf16[16,32,64,64]{2,3,1,0:T(8,128)(2,1)S(1)}, bf16[16,32,64,64]{2,3,1,0:T(8,128)(2,1)}) fusion(f32[16,32,128,128]{2,3,1,0:T(8,128)} %fusion.4), kind=kLoop, calls=%fused_computation.7 | loop fusion | flops 8388608 | bytes 41943040 | tf_op jit(solution)/shard_map/convert.7
  301.4 9.3 fusion.18
  310.8 12.2 %copy.79 = bf16[16,32,64,128]{3,1,0,2:T(8,128)(2,1)} copy(bf16[16,32,64,128]{3,2,1,0:T(8,128)(2,1)} %fusion.18) | data formatting | bytes 16777216 | tf_op jit(solution)/shard_map/convert_element_type | solution.py:71
  322.9 6.6 all-to-all-start.1
  329.6 13.5 %fusion.51 = (bf16[16,16,16,8,64]{4,3,2,1,0:T(8,128)(2,1)}, bf16[16,16,16,8,64]{4,3,2,1,0:T(8,128)(2,1)}) fusion(bf16[16,16,16,8,128]{4,3,2,1,0:T(8,128)(2,1)} %bitcast.86), kind=kLoop, calls=%fused_computation.65 | loop fusion | bytes 16777216 | tf_op jit(solution)/shard_map/slice | solution.py:79
  343.1 32.8 %copy.120 = bf16[16,16,16,8,64]{1,0,2,4,3:T(8,128)(2,1)} copy(bf16[16,16,16,8,64]{4,3,2,1,0:T(8,128)(2,1)} %get-tuple-element.10) | data formatting | bytes 8388608
  375.8 32.8 %copy.122 = bf16[16,16,16,8,64]{1,0,2,4,3:T(8,128)(2,1)} copy(bf16[16,16,16,8,64]{4,3,2,1,0:T(8,128)(2,1)} %get-tuple-element.9) | data formatting | bytes 8388608
  408.7 101.3 %all-to-all-done.1 = bf16[16,32,64,128]{3,1,0,2:T(8,128)(2,1)} async-done(((bf16[16,32,64,128]{3,1,0,2:T(8,128)(2,1)}), bf16[16,32,64,128]{3,1,0,2:T(8,128)(2,1)}, u32[]{:S(2)}, u32[]{:S(2)}) %all-to-all-start.1) | async-done | bytes 8388640 | tf_op jit(solution)/shard_map/all_to_all | solution.py:72
  509.9 16.5 %copy.81 = bf16[16,8,32,8,128]{4,3,2,1,0:T(8,128)(2,1)} copy(bf16[16,8,32,8,128]{4,2,0,3,1:T(8,128)(2,1)} %bitcast.15) | data formatting | bytes 16777216 | tf_op jit(solution)/shard_map/all_to_all | solution.py:72
  526.4 13.7 %fusion.52 = (bf16[16,16,16,8,64]{4,3,2,1,0:T(8,128)(2,1)}, bf16[16,16,16,8,64]{4,3,2,1,0:T(8,128)(2,1)}) fusion(bf16[16,16,16,8,128]{4,3,2,1,0:T(8,128)(2,1)} %bitcast.87), kind=kLoop, calls=%fused_computation.66 | loop fusion | bytes 16777216 | tf_op jit(solution)/shard_map/slice | solution.py:76
  540.1 33.3 %copy.119 = bf16[16,16,16,8,64]{0,1,2,4,3:T(8,128)(2,1)} copy(bf16[16,16,16,8,64]{4,3,2,1,0:T(8,128)(2,1)} %get-tuple-element.11) | data formatting | bytes 8388608
  573.4 33.4 %copy.121 = bf16[16,16,16,8,64]{0,1,2,4,3:T(8,128)(2,1)} copy(bf16[16,16,16,8,64]{4,3,2,1,0:T(8,128)(2,1)} %get-tuple-element.12) | data formatting | bytes 8388608
  606.8 27.0 %fusion.53 = f32[8,64,16,16,1]{3,2,4,1,0:T(8,128)S(1)} fusion(bf16[16,16,16,8,64]{0,1,2,4,3:T(8,128)(2,1)} %copy.119, bf16[16,16,16,8,64]{1,0,2,4,3:T(8,128)(2,1)} %copy.120), kind=kOutput, calls=%fused_computation.67 | convolution fusion | flops 67108864 | bytes 8912896 | tf_op jit(solution)/shard_map/uacxw,ubcxw->abxw/dot_general | solution.py:83
  633.8 29.1 %fusion.54 = f32[8,64,16,16,1]{3,2,4,1,0:T(8,128)} fusion(bf16[16,16,16,8,64]{0,1,2,4,3:T(8,128)(2,1)} %copy.121, bf16[16,16,16,8,64]{1,0,2,4,3:T(8,128)(2,1)} %copy.120), kind=kOutput, calls=%fused_computation.68 | convolution fusion | flops 67108864 | bytes 8912896 | tf_op jit(solution)/shard_map/uacxw,ubcxw->abxw/dot_general | solution.py:83
  662.9 26.6 %fusion.26 = f32[16,16,8,64]{1,0,3,2:T(8,128)} fusion(f32[8,64,16,16,1]{3,2,4,1,0:T(8,128)S(1)} %fusion.53, bf16[16,16,16,8,64]{0,1,2,4,3:T(8,128)(2,1)} %copy.121, bf16[16,16,16,8,64]{1,0,2,4,3:T(8,128)(2,1)} %copy.122), kind=kOutput, calls=%fused_computation.32 | convolution fusion | flops 67239936 | bytes 9437184 | tf_op jit(solution)/shard_map/uacxw,ubcxw->abxw/dot_general | solution.py:83
  692.4 30.6 %fusion.25 = f32[16,16,8,64]{1,0,3,2:T(8,128)} fusion(f32[8,64,16,16,1]{3,2,4,1,0:T(8,128)} %fusion.54, bf16[16,16,16,8,64]{0,1,2,4,3:T(8,128)(2,1)} %copy.119, bf16[16,16,16,8,64]{1,0,2,4,3:T(8,128)(2,1)} %copy.122), kind=kOutput, calls=%fused_computation.30 | convolution fusion | flops 67239936 | bytes 9437184 | tf_op jit(solution)/shard_map/uacxw,ubcxw->abxw/dot_general | solution.py:83
  727.2 32.6 %copy.89 = bf16[16,16,16,8,64]{2,1,0,4,3:T(8,128)(2,1)} copy(bf16[16,16,16,8,64]{4,3,2,1,0:T(8,128)(2,1)} %get-tuple-element.10) | data formatting | bytes 8388608 | tf_op jit(solution)/shard_map/slice | solution.py:78
  759.8 32.6 %copy.91 = bf16[16,16,16,8,64]{2,1,0,4,3:T(8,128)(2,1)} copy(bf16[16,16,16,8,64]{4,3,2,1,0:T(8,128)(2,1)} %get-tuple-element.9) | data formatting | bytes 8388608 | tf_op jit(solution)/shard_map/slice | solution.py:79
  797.5 33.9 %fusion.55 = f32[8,64,16,16,16]{4,2,3,1,0:T(8,128)} fusion(bf16[16,16,8,64,1]{1,0,4,3,2:T(8,128)(2,1)} %copy.105, bf16[16,16,16,8,64]{2,1,0,4,3:T(8,128)(2,1)} %copy.89), kind=kOutput, calls=%fused_computation.69 | convolution fusion | flops 67108864 | bytes 12845056 | tf_op jit(solution)/shard_map/abxw,ubcxw->uacxw/dot_general | solution.py:96
  831.4 33.9 %fusion.56 = f32[8,64,16,16,16]{4,2,3,1,0:T(8,128)} fusion(bf16[16,16,8,64,1]{1,0,4,3,2:T(8,128)(2,1)} %copy.105, bf16[16,16,16,8,64]{2,1,0,4,3:T(8,128)(2,1)} %copy.91), kind=kOutput, calls=%fused_computation.70 | convolution fusion | flops 67108864 | bytes 12845056 | tf_op jit(solution)/shard_map/abxw,ubcxw->uacxw/dot_general | solution.py:96
  865.3 43.4 %fusion = bf16[16,16,16,8,64]{2,1,0,4,3:T(8,128)(2,1)} fusion(f32[8,64,16,16,16]{4,2,3,1,0:T(8,128)} %fusion.55, bf16[16,16,8,64,1]{1,0,4,3,2:T(8,128)(2,1)S(1)} %copy.106, bf16[16,16,16,8,64]{2,1,0,4,3:T(8,128)(2,1)} %copy.91), kind=kOutput, calls=%fused_computation.2 | convolution fusion | flops 71303168 | bytes 17039360 | tf_op jit(solution)/shard_map/abxw,ubcxw->uacxw/dot_general | solution.py:96
  908.7 35.7 %copy.92 = bf16[16,16,16,8,64]{4,3,2,1,0:T(8,128)(2,1)} copy(bf16[16,16,16,8,64]{2,1,0,4,3:T(8,128)(2,1)} %fusion) | data formatting | bytes 8388608 | tf_op jit(solution)/shard_map/sub | solution.py:98
  944.4 43.3 %fusion.1 = bf16[16,16,16,8,64]{2,1,0,4,3:T(8,128)(2,1)} fusion(f32[8,64,16,16,16]{4,2,3,1,0:T(8,128)} %fusion.56, bf16[16,16,8,64,1]{1,0,4,3,2:T(8,128)(2,1)S(1)} %copy.106, bf16[16,16,16,8,64]{2,1,0,4,3:T(8,128)(2,1)} %copy.89), kind=kOutput, calls=%fused_computation.3 | convolution fusion | flops 71303168 | bytes 17039360 | tf_op jit(solution)/shard_map/abxw,ubcxw->uacxw/dot_general | solution.py:96
  987.7 35.7 %copy.97 = bf16[16,16,16,8,64]{4,3,2,1,0:T(8,128)(2,1)} copy(bf16[16,16,16,8,64]{2,1,0,4,3:T(8,128)(2,1)} %fusion.1) | data formatting | bytes 8388608 | tf_op jit(solution)/shard_map/add | solution.py:99
  1023.4 10.9 %pad_maximum_fusion = bf16[16,256,8,128]{3,2,1,0:T(8,128)(2,1)} fusion(bf16[16,256,8,64]{3,2,1,0:T(8,128)(2,1)} %bitcast.89, bf16[16,256,8,64]{3,2,1,0:T(8,128)(2,1)} %bitcast.88), kind=kLoop, calls=%fused_computation.21 | loop fusion | flops 16777216 | bytes 16777216 | tf_op jit(solution)/shard_map/concatenate | solution.py:100
  (14 shorter events, 12.5 us)
Async XLA Ops:
  15.7 186.2 %all-to-all-start = ((bf16[16,256,8,128]{3,2,0,1:T(8,128)(2,1)}), bf16[16,256,8,128]{3,2,0,1:T(8,128)(2,1)}, u32[]{:S(2)}, u32[]{:S(2)}) async-start(bf16[16,256,8,128]{3,2,0,1:T(8,128)(2,1)} %copy.76), calls=%async_computation | async-start | bytes 16777216 | tf_op jit(solution)/shard_map/all_to_all | solution.py:43
  322.9 187.0 %all-to-all-start.1 = ((bf16[16,32,64,128]{3,1,0,2:T(8,128)(2,1)}), bf16[16,32,64,128]{3,1,0,2:T(8,128)(2,1)}, u32[]{:S(2)}, u32[]{:S(2)}) async-start(bf16[16,32,64,128]{3,1,0,2:T(8,128)(2,1)} %copy.79), calls=%async_computation.1 | async-start | bytes 16777216 | tf_op jit(solution)/shard_map/all_to_all | solution.py:72
  329.6 462.8 %all-reduce.2.cloned.1.call-start = ((), (), s32[]{:S(2)}) async-start(), calls=%async_computation.2 | async-start | bytes 2097152 | tf_op jit(solution)/shard_map/psum | solution.py:89
  759.8 32.6 %copy-start = (f32[256,8,128]{2,1,0:T(8,128)S(1)}, f32[256,8,128]{2,1,0:T(8,128)}, u32[]{:S(2)}) copy-start(f32[256,8,128]{2,1,0:T(8,128)} %param.5) | copy-start | bytes 3145732
Sparse Core Ops, SparseCore 0:
  727.3 37.4 all-reduce.1
where the time goes:
time: 1060 us; the launch traced here: 1040 us
  local copies, waits for them, and re-layouts  343 us (32%)
  matrix products  310 us (29%)
  waiting for transfers between devices  270 us (25%)
  other arithmetic  92.1 us (9%)
  between operations  13.6 us (1%)
  starting transfers between devices  12.3 us (1%)
    all_to_all x1, waiting for transfers between devices, on_device(): lax.all_to_all(green_row, 'ka', split_axis=1, concat_axis=2, tiled=True)  169 us
    dot_general x4, matrix products, apply_kernel(): jnp.einsum(apply_form, left, right, preferred_element_type=jnp.float32)  154 us
    unnamed x7, local copies, waits for them, and re-layouts  141 us
    dot_general x4, matrix products, contract(): return jnp.einsum(form, left, right, preferred_element_type=jnp.float32)  113 us
    all_to_all x1, waiting for transfers between devices, on_device(): lax.all_to_all(sigma_pairs, 'ka', split_axis=2, concat_axis=1, tiled=True)  101 us
    another operation x2, other arithmetic  67 us
    slice x2, local copies, waits for them, and re-layouts, on_device(): green_im = green[..., half_width:]  46.1 us
    add x1, local copies, waits for them, and re-layouts, on_device(): apply_kernel(kernel_re, green_im) + apply_kernel(kernel_im, green_re)  35.7 us
  transfers between devices with their start and end apart: 3, of which 2 were waited for; matrix products, arithmetic and copies ran while one was open for 15% of the time, Pallas kernels for 0%

commit v1 on v0

--- a/solution.py
+++ b/solution.py
@@ -1,13 +1,17 @@
+import functools
 import math
 
 import jax
 import jax.numpy as jnp
 from jax import lax
+from jax.experimental import pallas as pl
+from jax.experimental.pallas import tpu as pltpu
 from jax.sharding import PartitionSpec as P
 
 NO = 16
 NKX = 64
 NKY = 64
+VMEM_LIMIT = 58 * 1024 * 1024
 
 
 step_size = 0.004
@@ -31,7 +35,317 @@
     return jnp.concatenate([upper, lower], axis=0)
 
 
-def on_device(green_row, screened, propagator):
+def swap_columns(matrix):
+    half = matrix.shape[1] // 2
+    return jnp.concatenate([matrix[:, half:], matrix[:, :half]], axis=1)
+
+
+def params(**more):
+    return pltpu.CompilerParams(vmem_limit_bytes=VMEM_LIMIT, **more)
+
+
+def cost(flops, bytes_accessed):
+    return pl.CostEstimate(flops=flops, bytes_accessed=bytes_accessed, transcendentals=0)
+
+
+def screened_block(field, screen_ref, forward_ref, inverse_ref, u, first, group, parts):
+    full_x, width = screen_ref.shape[2:]
+    xl = full_x // parts
+    middle = width // 2
+    low = lax.broadcasted_iota(jnp.int32, (full_x, width), 1) < middle
+    field = field.astype(jnp.float32).reshape(parts, group, xl, width)
+    backs = []
+    for pair in range(0, group, 2):
+        columns = []
+        for k in (pair, pair + 1):
+            x = field[:, k].reshape(full_x, width)
+            turned = pltpu.roll(x, middle, 1)
+            turned = jnp.where(low, -turned, turned)
+            columns.append(jnp.concatenate([x, turned], axis=0).astype(jnp.bfloat16))
+        stacked = jnp.concatenate(columns, axis=1)
+        space = jnp.dot(forward_ref[...], stacked, preferred_element_type=jnp.float32)
+        columns = []
+        for j in range(2):
+            s = space[:, j * width : (j + 1) * width]
+            w = screen_ref[u, first + pair + j].astype(jnp.float32)
+            direct = s * w
+            crossed = s * pltpu.roll(w, middle, 1)
+            moved = pltpu.roll(jnp.where(low, crossed, -direct), middle, 1)
+            prod = jnp.where(low, direct, crossed) + moved
+            turned = pltpu.roll(prod, middle, 1)
+            turned = jnp.where(low, -turned, turned)
+            columns.append(jnp.concatenate([prod, turned], axis=0).astype(jnp.bfloat16))
+        stacked = jnp.concatenate(columns, axis=1)
+        back = jnp.dot(inverse_ref[...], stacked, preferred_element_type=jnp.float32)
+        for j in range(2):
+            backs.append(back[:, j * width : (j + 1) * width].reshape(parts, 1, xl, width))
+    out = jnp.concatenate(backs, axis=1).reshape(parts, group * xl, width)
+    return out.astype(jnp.bfloat16)
+
+
+def time_kernel(parts, hist, green, screened, base, forward_y, inverse_y, spread, forward_x, inverse_x):
+    steps, rows, width = green.shape
+    pairs = screened.shape[1]
+    piece = rows // parts
+    xl = rows // (NO * NO)
+    group = min(16, pairs)
+    ta, tb = 4, 8
+    quarter = NO // hist
+    qrows = rows // hist
+    mesh_id = pl.DeviceIdType.MESH
+
+    def body(
+        green_ref, screen_ref, base_ref, fy_ref, iy_ref, spread_ref, fx_ref, ix_ref, out_ref,
+        send, there, here, sig, gre, total, sums, final, send_sem, recv_sem, hsend_sem, hrecv_sem,
+    ):
+        me = lax.axis_index("ka")
+        mine = lax.axis_index("ha")
+        barrier = pltpu.get_barrier_semaphore()
+        for k in range(1, parts):
+            pl.semaphore_signal(
+                barrier, inc=1, device_id={"ka": lax.rem(me + k, parts)}, device_id_type=mesh_id
+            )
+        for k in range(1, hist):
+            pl.semaphore_signal(
+                barrier, inc=1, device_id={"ha": lax.rem(mine + k, hist)}, device_id_type=mesh_id
+            )
+        pl.semaphore_wait(barrier, parts + hist - 2)
+
+        def spread_out(phase, source, target, u):
+            target[u, me] = source[u, me]
+            for k in range(1, parts):
+                other = lax.rem(me + k, parts)
+                pltpu.make_async_remote_copy(
+                    src_ref=source.at[u, other],
+                    dst_ref=target.at[u, me],
+                    send_sem=send_sem.at[phase, u],
+                    recv_sem=recv_sem.at[phase, u],
+                    device_id={"ka": other},
+                    device_id_type=mesh_id,
+                ).start()
+
+        def wait_for(ref, count, sem):
+            pltpu.make_async_copy(ref.at[pl.ds(0, count)], ref.at[pl.ds(0, count)], sem).wait()
+
+        def forward(u, carry):
+            half = jnp.dot(green_ref[u], fy_ref[...], preferred_element_type=jnp.float32)
+            send[u] = half.astype(jnp.bfloat16).reshape(parts, piece, width)
+            spread_out(0, send, there, u)
+            return carry
+
+        lax.fori_loop(0, steps, forward, 0)
+
+        def screen(u, carry):
+            wait_for(there.at[u], parts - 1, recv_sem.at[0, u])
+
+            def block(j, inner):
+                at = pl.ds(pl.multiple_of(j * (group * xl), group * xl), group * xl)
+                there[u, :, at] = screened_block(
+                    there[u, :, at], screen_ref, fx_ref, ix_ref, u, j * group, group, parts
+                )
+                return inner
+
+            lax.fori_loop(0, pairs // group, block, 0)
+            spread_out(1, there, here, u)
+            return carry
+
+        lax.fori_loop(0, steps, screen, 0)
+        total[...] = jnp.zeros(total.shape, jnp.float32)
+
+        def remember(u, carry):
+            values = jnp.dot(green_ref[u], spread_ref[...], preferred_element_type=jnp.float32)
+            gre[0] = values[:, :width].reshape(NO, NO, xl, width)
+            gre[1] = values[:, width:].reshape(NO, NO, xl, width)
+            wait_for(here.at[u], parts - 1, recv_sem.at[1, u])
+            values = jnp.dot(
+                here[u].reshape(rows, width), iy_ref[...], preferred_element_type=jnp.float32
+            )
+            sig[0] = values[:, :width].reshape(NO, NO, xl, width)
+            sig[1] = values[:, width:].reshape(NO, NO, xl, width)
+
+            def tile(n, inner):
+                a0 = n // (NO // tb) * ta
+                b0 = n % (NO // tb) * tb
+                acc = [[total[a0 + i, b0 + j] for j in range(tb)] for i in range(ta)]
+                for c in range(NO):
+                    s = [sig[0, a0 + i, c] for i in range(ta)]
+                    t = [sig[1, a0 + i, c] for i in range(ta)]
+                    for j in range(tb):
+                        g = gre[0, b0 + j, c]
+                        h = gre[1, b0 + j, c]
+                        for i in range(ta):
+                            acc[i][j] = acc[i][j] + s[i] * g + t[i] * h
+                for i in range(ta):
+                    for j in range(tb):
+                        total[a0 + i, b0 + j] = acc[i][j]
+                return inner
+
+            lax.fori_loop(0, NO * NO // (ta * tb), tile, 0)
+            return carry
+
+        lax.fori_loop(0, steps, remember, 0)
+
+        for k in range(1, hist):
+            other = lax.rem(mine + k, hist)
+            pltpu.make_async_remote_copy(
+                src_ref=total.at[pl.ds(other * quarter, quarter)],
+                dst_ref=sums.at[mine],
+                send_sem=hsend_sem.at[0],
+                recv_sem=hrecv_sem.at[0],
+                device_id={"ha": other},
+                device_id_type=mesh_id,
+            ).start()
+        sums[mine] = total[pl.ds(mine * quarter, quarter)]
+        wait_for(sums, hist - 1, hrecv_sem.at[0])
+        whole = sums[0]
+        for k in range(1, hist):
+            whole = whole + sums[k]
+        at = pl.ds(pl.multiple_of(mine * qrows, qrows), qrows)
+        kernel = base_ref[at] + step_size * whole.reshape(qrows, width)
+        final[mine] = kernel.astype(jnp.bfloat16)
+        for k in range(1, hist):
+            other = lax.rem(mine + k, hist)
+            pltpu.make_async_remote_copy(
+                src_ref=final.at[mine],
+                dst_ref=final.at[mine],
+                send_sem=hsend_sem.at[1],
+                recv_sem=hrecv_sem.at[1],
+                device_id={"ha": other},
+                device_id_type=mesh_id,
+            ).start()
+        wait_for(final, hist - 1, hrecv_sem.at[1])
+        out_ref[...] = final[...].reshape(rows, width)
+        wait_for(sums, hist - 1, hsend_sem.at[0])
+        wait_for(final, hist - 1, hsend_sem.at[1])
+
+        def drain(u, carry):
+            wait_for(send.at[u], parts - 1, send_sem.at[0, u])
+            wait_for(there.at[u], parts - 1, send_sem.at[1, u])
+            return carry
+
+        lax.fori_loop(0, steps, drain, 0)
+
+    blocks = pltpu.VMEM((steps, parts, piece, width), jnp.bfloat16)
+    field = pltpu.VMEM((2, NO, NO, xl, width), jnp.float32)
+    return pl.pallas_call(
+        body,
+        in_specs=[pl.BlockSpec(memory_space=pltpu.VMEM)] * 8,
+        out_specs=pl.BlockSpec(memory_space=pltpu.VMEM),
+        out_shape=jax.ShapeDtypeStruct((rows, width), jnp.bfloat16),
+        scratch_shapes=[
+            blocks,
+            blocks,
+            blocks,
+            field,
+            field,
+            pltpu.VMEM((NO, NO, xl, width), jnp.float32),
+            pltpu.VMEM((hist, quarter, NO, xl, width), jnp.float32),
+            pltpu.VMEM((hist, qrows, width), jnp.bfloat16),
+            pltpu.SemaphoreType.DMA((2, steps)),
+            pltpu.SemaphoreType.DMA((2, steps)),
+            pltpu.SemaphoreType.DMA((2,)),
+            pltpu.SemaphoreType.DMA((2,)),
+        ],
+        compiler_params=params(collective_id=0, has_side_effects=True),
+        cost_estimate=cost(100 * steps * rows * width * width, 4 * steps * rows * width),
+        name="time_kernel",
+    )(green, screened, base, forward_y, inverse_y, spread, forward_x, inverse_x)
+
+
+def advance(kernel, green, spread):
+    steps, rows, width = green.shape
+    xl = rows // (NO * NO)
+    middle = width // 2
+    ta, tc = 4, 8
+
+    def body(kernel_ref, green_ref, spread_ref, out_ref, ker, gre, new):
+        @pl.when(pl.program_id(0) == 0)
+        def _():
+            low = lax.broadcasted_iota(jnp.int32, (rows, width), 1) < middle
+            kernel = kernel_ref[...].astype(jnp.float32)
+            turned = pltpu.roll(kernel, middle, 1)
+            ker[0] = jnp.where(low, kernel, turned).reshape(NO, NO, xl, width)
+            ker[1] = jnp.where(low, -turned, kernel).reshape(NO, NO, xl, width)
+
+        values = jnp.dot(green_ref[0], spread_ref[...], preferred_element_type=jnp.float32)
+        gre[0] = values[:, :width].reshape(NO, NO, xl, width)
+        gre[1] = values[:, width:].reshape(NO, NO, xl, width)
+
+        def tile(n, carry):
+            a0 = n // (NO // tc) * ta
+            c0 = n % (NO // tc) * tc
+            acc = [[jnp.zeros((xl, width), jnp.float32) for j in range(tc)] for i in range(ta)]
+            for b in range(NO):
+                s = [ker[0, a0 + i, b] for i in range(ta)]
+                t = [ker[1, a0 + i, b] for i in range(ta)]
+                for j in range(tc):
+                    g = gre[0, b, c0 + j]
+                    h = gre[1, b, c0 + j]
+                    for i in range(ta):
+                        acc[i][j] = acc[i][j] + s[i] * g + t[i] * h
+            for i in range(ta):
+                for j in range(tc):
+                    new[a0 + i, c0 + j] = acc[i][j]
+            return carry
+
+        lax.fori_loop(0, NO * NO // (ta * tc), tile, 0)
+        out_ref[0] = new[...].reshape(rows, width).astype(jnp.bfloat16)
+
+    return pl.pallas_call(
+        body,
+        grid=(steps,),
+        in_specs=[
+            pl.BlockSpec((rows, width), lambda i: (0, 0)),
+            pl.BlockSpec((1, rows, width), lambda i: (i, 0, 0)),
+            pl.BlockSpec((width, 2 * width), lambda i: (0, 0)),
+        ],
+        out_specs=pl.BlockSpec((1, rows, width), lambda i: (i, 0, 0)),
+        out_shape=jax.ShapeDtypeStruct(green.shape, jnp.bfloat16),
+        scratch_shapes=[
+            pltpu.VMEM((2, NO, NO, xl, width), jnp.float32),
+            pltpu.VMEM((2, NO, NO, xl, width), jnp.float32),
+            pltpu.VMEM((NO, NO, xl, width), jnp.float32),
+        ],
+        compiler_params=params(),
+        cost_estimate=cost(40 * steps * rows * width * width, 4 * steps * rows * width),
+        name="advance",
+    )(kernel, green, spread)
+
+
+def by_kernels(parts, hist, green_row, screened, propagator):
+    steps, pairs, xl, width = green_row.shape
+    middle = width // 2
+    rows = pairs * xl
+    cos_y, sin_y = tables(NKY)
+    cos_x, sin_x = tables(NKX)
+    forward_y = row_matrix(cos_y, sin_y, True)
+    inverse_y = row_matrix(cos_y, sin_y, False)
+    inverse_y = jnp.concatenate([inverse_y, swap_columns(inverse_y)], axis=1)
+    forward_x = jnp.concatenate([cos_x, sin_x], axis=1)
+    inverse_x = jnp.concatenate([cos_x, -sin_x], axis=1)
+    one = jnp.eye(width, dtype=jnp.bfloat16)
+    real, imag = one[:, :middle], one[:, middle:]
+    conjugate = jnp.concatenate([real, real, imag, -imag], axis=1)
+    crossed = jnp.concatenate([real, imag, imag, real], axis=1)
+
+    green = green_row.reshape(steps, rows, width)
+    kernel = time_kernel(
+        parts,
+        hist,
+        green,
+        screened,
+        propagator.reshape(rows, width),
+        forward_y,
+        inverse_y,
+        conjugate,
+        forward_x,
+        inverse_x,
+    )
+    new = advance(kernel, green, crossed)
+    return new.reshape(steps, pairs, xl, width)
+
+
+def by_operations(green_row, screened, propagator):
     steps_local, pairs, rows_local, columns = green_row.shape
     half_width = columns // 2
     cos_y, sin_y = tables(NKY)
@@ -101,9 +415,20 @@
     return result.astype(jnp.bfloat16).reshape(steps_local, pairs, rows_local, columns)
 
 
+def on_device(parts, hist, green_row, screened, propagator):
+    steps, pairs, xl, width = green_row.shape
+    if xl % 8 or width != 128 or NO % hist or pairs % (2 * parts):
+        return by_operations(green_row, screened, propagator)
+    return by_kernels(parts, hist, green_row, screened, propagator)
+
+
 def solution(mesh):
     in_specs = (P("ha", None, "ka", None), P("ha", "ka", None, None), P(None, "ka", None))
     out_specs = P("ha", None, "ka", None)
     return jax.shard_map(
-        on_device, mesh=mesh, in_specs=in_specs, out_specs=out_specs, check_vma=False
+        functools.partial(on_device, mesh.shape["ka"], mesh.shape["ha"]),
+        mesh=mesh,
+        in_specs=in_specs,
+        out_specs=out_specs,
+        check_vma=False,
     )

time: 1060 us -> 446 us (0.42); the launches traced: 1040 us -> 446 us
  Pallas kernels: 0 us -> 442 us
  local copies, waits for them, and re-layouts: 343 us -> 0.08 us
  matrix products: 310 us -> 0 us
  waiting for transfers between devices: 270 us -> 0 us
  other arithmetic: 92.1 us -> 3.26 us
  between operations: 13.6 us -> 0.03 us
  starting transfers between devices: 12.3 us -> 0 us
    pallas_call x0 -> x2, Pallas kernels: none -> 442 us  [the longest x1 395 us: time_kernel(): pl.pallas_call(body, in_specs=[pl.BlockSpec(memory_space=pltpu.VMEM)] * 8...]
    dot_general x11 -> x0, matrix products: 310 us -> none  [the longest x4 154 us: apply_kernel(): jnp.einsum(apply_form, left, right, preferred_element_type=jnp.float32)]
    all_to_all x2 -> x0, waiting for transfers between devices: 270 us -> none  [the longest x1 169 us: on_device(): lax.all_to_all(green_row, 'ka', split_axis=1, concat_axis=2, tiled=True)]
    unnamed x7 -> x0, local copies, waits for them, and re-layouts: 141 us -> none
    slice x7 -> x1, local copies, waits for them, and re-layouts: 96.2 us -> 0.08 us  [swap_columns(): return jnp.concatenate([matrix[:, half:], matrix[:, :half]], axis=1)]
    another operation x2 -> x0, other arithmetic: 67 us -> none
    add x2 -> x0, local copies, waits for them, and re-layouts: 38.6 us -> none  [the longest x1 35.7 us: on_device(): apply_kernel(kernel_re, green_im) + apply_kernel(kernel_im, green_re)]
    sub x2 -> x0, local copies, waits for them, and re-layouts: 38.6 us -> none  [the longest x1 35.7 us: on_device(): apply_kernel(kernel_re, green_re) - apply_kernel(kernel_im, green_im)]
  transfers between devices with their start and end apart: 3 -> 0, of which waited for: 2 -> 0; matrix products, arithmetic and copies ran while one was open for 15% -> 0% of each run, Pallas kernels for 0% -> 0%
where the time goes in v1:
time: 446 us
  Pallas kernels  442 us (99%)
    pallas_call x1, Pallas kernels, time_kernel(): pl.pallas_call(body, in_specs=[pl.BlockSpec(memory_space=pltpu.VMEM)] * 8...  395 us
    pallas_call x1, Pallas kernels, advance(): pl.pallas_call(body, grid=(steps,), in_specs=[pl.BlockSpec((rows, width),...  47.8 us

profile of v1, /device:TPU:11, one launch (start us, length us, event | category | flops | bytes accessed | tf_op | source)
XLA Modules:
  0.0 445.8 jit_solution(7599349010536946407)
XLA Ops:
  0.0 0.1 fusion.9
  0.2 0.2 multiply_convert_fusion
  0.3 0.7 pad_maximum_fusion.8
  1.0 0.7 fusion.2
  1.7 0.1 fusion.11
  1.8 0.7 pad_maximum_fusion.iy_ref
  2.5 0.1 fusion.10
  2.6 0.8 pad_maximum_fusion.2
  3.4 394.6 %time_kernel.1.kernel_ref = bf16[2048,128]{1,0:T(8,128)(2,1)} custom-call(bf16[16,2048,128]{2,1,0:T(8,128)(2,1)} %bitcast.3, bf16[16,32,64,128]{3,2,1,0:T(8,128)(2,1)} %screen_ref.1, f32[2048,128]{1,0:T(8,128)} %bitcast.5, bf16[128,128]{1,0:T(8,128)(2,1)} %get-tuple-element.8.fy_ref, bf16[128,256]{1,0:T(8,128)(2,1)} %pad_maximum_fusion.iy_ref, ...), custom_call_target="tpu_custom_call" | custom-call | flops 53687091200 | bytes 16777216 | tf_op jit(solution)/shard_map/time_kernel/pallas_call | solution.py:230
  398.0 47.8 %advance.1 = bf16[16,2048,128]{2,1,0:T(8,128)(2,1)} custom-call(bf16[2048,128]{1,0:T(8,128)(2,1)} %time_kernel.1.kernel_ref, bf16[16,2048,128]{2,1,0:T(8,128)(2,1)} %bitcast.4, bf16[128,256]{1,0:T(8,128)(2,1)} %get-tuple-element.5.spread_ref), custom_call_target="tpu_custom_call" | custom-call | flops 21474836480 | bytes 16777216 | tf_op jit(solution)/shard_map/advance/pallas_call | solution.py:294
  (1 shorter events, 0.0 us)

commit v2 on v1

--- a/solution.py
+++ b/solution.py
@@ -95,9 +95,12 @@
     mesh_id = pl.DeviceIdType.MESH
 
     def body(
-        green_ref, screen_ref, base_ref, fy_ref, iy_ref, spread_ref, fx_ref, ix_ref, out_ref,
+        green_ref, screen_hbm, base_ref, fy_ref, iy_ref, spread_ref, fx_ref, ix_ref, out_ref,
         send, there, here, sig, gre, total, sums, final, send_sem, recv_sem, hsend_sem, hrecv_sem,
+        screen_ref, load_sem,
     ):
+        load = pltpu.make_async_copy(screen_hbm, screen_ref, load_sem)
+        load.start()
         me = lax.axis_index("ka")
         mine = lax.axis_index("ha")
         barrier = pltpu.get_barrier_semaphore()
@@ -149,6 +152,7 @@
             spread_out(1, there, here, u)
             return carry
 
+        load.wait()
         lax.fori_loop(0, steps, screen, 0)
         total[...] = jnp.zeros(total.shape, jnp.float32)
 
@@ -229,7 +233,7 @@
     field = pltpu.VMEM((2, NO, NO, xl, width), jnp.float32)
     return pl.pallas_call(
         body,
-        in_specs=[pl.BlockSpec(memory_space=pltpu.VMEM)] * 8,
+        in_specs=[pl.BlockSpec(memory_space=pl.ANY if k == 1 else pltpu.VMEM) for k in range(8)],
         out_specs=pl.BlockSpec(memory_space=pltpu.VMEM),
         out_shape=jax.ShapeDtypeStruct((rows, width), jnp.bfloat16),
         scratch_shapes=[
@@ -245,6 +249,8 @@
             pltpu.SemaphoreType.DMA((2, steps)),
             pltpu.SemaphoreType.DMA((2,)),
             pltpu.SemaphoreType.DMA((2,)),
+            pltpu.VMEM(screened.shape, screened.dtype),
+            pltpu.SemaphoreType.DMA,
         ],
         compiler_params=params(collective_id=0, has_side_effects=True),
         cost_estimate=cost(100 * steps * rows * width * width, 4 * steps * rows * width),
@@ -258,7 +264,12 @@
     middle = width // 2
     ta, tc = 4, 8
 
-    def body(kernel_ref, green_ref, spread_ref, out_ref, ker, gre, new):
+    tiles = NO * NO // (ta * tc)
+    share = NO // tiles
+
+    def body(kernel_ref, green_ref, next_ref, spread_ref, out_ref, ker, gre):
+        now = pl.program_id(0) % 2
+
         @pl.when(pl.program_id(0) == 0)
         def _():
             low = lax.broadcasted_iota(jnp.int32, (rows, width), 1) < middle
@@ -267,29 +278,34 @@
             ker[0] = jnp.where(low, kernel, turned).reshape(NO, NO, xl, width)
             ker[1] = jnp.where(low, -turned, kernel).reshape(NO, NO, xl, width)
 
-        values = jnp.dot(green_ref[0], spread_ref[...], preferred_element_type=jnp.float32)
-        gre[0] = values[:, :width].reshape(NO, NO, xl, width)
-        gre[1] = values[:, width:].reshape(NO, NO, xl, width)
+            values = jnp.dot(green_ref[0], spread_ref[...], preferred_element_type=jnp.float32)
+            gre[0, 0] = values[:, :width].reshape(NO, NO, xl, width)
+            gre[0, 1] = values[:, width:].reshape(NO, NO, xl, width)
 
         def tile(n, carry):
             a0 = n // (NO // tc) * ta
             c0 = n % (NO // tc) * tc
+            part = pl.ds(pl.multiple_of(n * (rows // tiles), rows // tiles), rows // tiles)
+            values = jnp.dot(next_ref[0, part], spread_ref[...], preferred_element_type=jnp.float32)
+            shape = (share, NO, xl, width)
+            gre[1 - now, 0, pl.ds(n * share, share)] = values[:, :width].reshape(shape)
+            gre[1 - now, 1, pl.ds(n * share, share)] = values[:, width:].reshape(shape)
             acc = [[jnp.zeros((xl, width), jnp.float32) for j in range(tc)] for i in range(ta)]
             for b in range(NO):
                 s = [ker[0, a0 + i, b] for i in range(ta)]
                 t = [ker[1, a0 + i, b] for i in range(ta)]
                 for j in range(tc):
-                    g = gre[0, b, c0 + j]
-                    h = gre[1, b, c0 + j]
+                    g = gre[now, 0, b, c0 + j]
+                    h = gre[now, 1, b, c0 + j]
                     for i in range(ta):
                         acc[i][j] = acc[i][j] + s[i] * g + t[i] * h
             for i in range(ta):
-                for j in range(tc):
-                    new[a0 + i, c0 + j] = acc[i][j]
+                at = pl.multiple_of(((a0 + i) * NO + c0) * xl, tc * xl)
+                tile_rows = jnp.concatenate(acc[i], axis=0).astype(jnp.bfloat16)
+                out_ref[0, pl.ds(at, tc * xl)] = tile_rows
             return carry
 
-        lax.fori_loop(0, NO * NO // (ta * tc), tile, 0)
-        out_ref[0] = new[...].reshape(rows, width).astype(jnp.bfloat16)
+        lax.fori_loop(0, tiles, tile, 0)
 
     return pl.pallas_call(
         body,
@@ -297,19 +313,19 @@
         in_specs=[
             pl.BlockSpec((rows, width), lambda i: (0, 0)),
             pl.BlockSpec((1, rows, width), lambda i: (i, 0, 0)),
+            pl.BlockSpec((1, rows, width), lambda i: (jnp.minimum(i + 1, steps - 1), 0, 0)),
             pl.BlockSpec((width, 2 * width), lambda i: (0, 0)),
         ],
         out_specs=pl.BlockSpec((1, rows, width), lambda i: (i, 0, 0)),
         out_shape=jax.ShapeDtypeStruct(green.shape, jnp.bfloat16),
         scratch_shapes=[
             pltpu.VMEM((2, NO, NO, xl, width), jnp.float32),
-            pltpu.VMEM((2, NO, NO, xl, width), jnp.float32),
-            pltpu.VMEM((NO, NO, xl, width), jnp.float32),
+            pltpu.VMEM((2, 2, NO, NO, xl, width), jnp.float32),
         ],
         compiler_params=params(),
         cost_estimate=cost(40 * steps * rows * width * width, 4 * steps * rows * width),
         name="advance",
-    )(kernel, green, spread)
+    )(kernel, green, green, spread)
 
 
 def by_kernels(parts, hist, green_row, screened, propagator):

time: 446 us -> 456 us (1.022)
  Pallas kernels: 442 us -> 452 us
    pallas_call x1, Pallas kernels: 47.8 us -> 59.8 us  [advance(): pl.pallas_call(body, grid=(steps,), in_specs=[pl.BlockSpec((rows, width),...]
where the time goes in v2:
time: 456 us
  Pallas kernels  452 us (99%)
    pallas_call x1, Pallas kernels, time_kernel(): pl.pallas_call(body, in_specs=[pl.BlockSpec(memory_space=pl.ANY if k == 1...  392 us
    pallas_call x1, Pallas kernels, advance(): pl.pallas_call(body, grid=(steps,), in_specs=[pl.BlockSpec((rows, width),...  59.8 us

profile of v2, /device:TPU:11, one launch (start us, length us, event | category | flops | bytes accessed | tf_op | source)
XLA Modules:
  0.0 455.6 jit_solution(18335143693459387938)
XLA Ops:
  0.0 0.1 fusion.9
  0.2 0.2 multiply_convert_fusion
  0.3 0.7 pad_maximum_fusion.8
  1.0 0.7 fusion.2
  1.7 0.1 fusion.11
  1.8 0.7 pad_maximum_fusion.iy_ref
  2.5 0.1 fusion.10
  2.6 0.8 pad_maximum_fusion.2
  3.4 392.4 %time_kernel.1.kernel_ref = bf16[2048,128]{1,0:T(8,128)(2,1)} custom-call(bf16[16,2048,128]{2,1,0:T(8,128)(2,1)} %bitcast.3, bf16[16,32,64,128]{3,2,1,0:T(8,128)(2,1)} %screen_hbm.1, f32[2048,128]{1,0:T(8,128)} %bitcast.6, bf16[128,128]{1,0:T(8,128)(2,1)} %get-tuple-element.8.fy_ref, bf16[128,256]{1,0:T(8,128)(2,1)} %pad_maximum_fusion.iy_ref, ...), custom_call_target="tpu_custom_call" | custom-call | flops 53687091200 | bytes 16777216 | tf_op jit(solution)/shard_map/time_kernel/pallas_call | solution.py:234
  395.8 59.8 %advance.1 = bf16[16,2048,128]{2,1,0:T(8,128)(2,1)} custom-call(bf16[2048,128]{1,0:T(8,128)(2,1)} %time_kernel.1.kernel_ref, bf16[16,2048,128]{2,1,0:T(8,128)(2,1)} %bitcast.4, bf16[16,2048,128]{2,1,0:T(8,128)(2,1)} %bitcast.5, bf16[128,256]{1,0:T(8,128)(2,1)} %get-tuple-element.5.spread_ref), custom_call_target="tpu_custom_call" | custom-call | flops 21474836480 | bytes 16777216 | tf_op jit(solution)/shard_map/advance/pallas_call | solution.py:310
  (1 shorter events, 0.0 us)
